TPU v7x, 128 devices: a whole 4x4x4 slice. The times are simulated.
128 devices in a mesh: role: 2 (over core), shard: 64 (over x, z, y).
Axes of the slice: x: 4, y: 4, z: 4, core: 2. Of those that a mesh axis runs over, the one named last changes fastest.
Arguments:
- feature_ids: int32 [2, 8, 4, 32768], P('role', None, None, 'shard'), may hold values from 0 to 3071
- labels: float32 [32768], P('shard'), may hold values from 0 to 1
- cold_rows: bfloat16 [2, 131072, 128], P('role', 'shard'), may hold values from -3 to 3
- hot_rows: bfloat16 [1024, 128], replicated, may hold values from -3 to 3
- block_owner: int32 [64, 64], P('shard'), may hold values from 0 to 63, as said below
- pushed: int32 [16384], P('shard'), may hold values from 0 to 1, as said below
- weight_in: bfloat16 [1024, 1024], replicated, may hold values from -0.1875 to 0.1875
- bias_in: bfloat16 [1024], replicated, may hold values from -3 to 3
- weight_out: bfloat16 [1024], replicated, may hold values from -0.1875 to 0.1875
Outputs:
- scores: float32 [2, 32768], P('role', 'shard')
- cold_after: bfloat16 [2, 131072, 128], P('role', 'shard')
- hot_after: bfloat16 [1024, 128], P('shard')
- weight_after: bfloat16 [1024, 1024], P('shard')
Inputs may be any that keep to these rules, and one draw needn't show every extreme that they name: `feature_ids`: an id below 1024 names that hot row; an id v of 1024 or more names row v - 1024 of the device's own share of cold rows (trainer share on role 0, serving share on role 1). `block_owner`: each row and each column holds every serving device once. `pushed`: in every draw some trainer has all 4 blocks of some group marked.
All inputs are finite; a program needn't handle non-finite values.
Results may differ from a plain program's by a relative error of at most 0.01.
Values may be sent and summed in bfloat16 or wider, within the bound.
A program may use at most 128 MiB of HBM per device.

v0:
```python
import math

import jax
import jax.numpy as jnp
from jax import lax
from jax.experimental import pallas as pl
from jax.experimental.pallas import tpu as pltpu
from jax.sharding import PartitionSpec as P

row_rate = 0.25
epsilon = 1e-06
unsent = 1e30
BF = jnp.bfloat16
F32 = jnp.float32
MESH = pl.DeviceIdType.MESH
NN = (((1,), (0,)), ((), ()))
NT = (((1,), (1,)), ((), ()))
TN = (((0,), (0,)), ((), ()))

SHARDS = 64
SLOTS = 8
BAGS = 4
N = 512
E = 128
H = 1024
HOT = 1024
COLD = 2048
TABLE = HOT + COLD
PIECE = H // SHARDS
BLK = 8
SPAN = 256


def dot(lhs, rhs, dims=NN):
    return lax.dot_general(lhs, rhs, dims, preferred_element_type=F32)


def sigmoid(value):
    return 0.5 * jnp.tanh(0.5 * value) + 0.5


def step_rows(old_rows, grad_rows):
    scale_rows = jnp.sqrt(jnp.mean(grad_rows * grad_rows, axis=-1, keepdims=True) + epsilon)
    return old_rows.astype(F32) - row_rate * grad_rows / scale_rows


def part(index, size):
    return pl.ds(pl.multiple_of(index * size, size), size)


def identity():
    rows = lax.broadcasted_iota(jnp.int32, (E, E), 0)
    return (rows == lax.broadcasted_iota(jnp.int32, (E, E), 1)).astype(F32).astype(BF)


def first_row(value):
    return lax.broadcasted_iota(jnp.int32, (16, N), 0) == 0


def slot_rows(ids, slot):
    own = [ids[slot, bag][None, :] for bag in range(BAGS)]
    mult = [sum((one == other).astype(F32) for other in own).astype(BF) for one in own]
    return own, mult


def count_block(own, mult, block):
    spots = lax.broadcasted_iota(jnp.int32, (SPAN, N), 0).astype(F32).astype(BF)
    acc = jnp.zeros((SPAN, N), BF)
    for bag in range(BAGS):
        at = jnp.clip(own[bag] - block * SPAN, -1, SPAN).astype(F32).astype(BF)
        acc = jnp.where(spots == at, mult[bag], acc)
    return acc


def round_kernel(
    ids, labels, hot, cold, weight, bias, wout, source, pushed,
    scores, cold_out, hot_after, weight_after,
    counts, table_t, pooled_t, pre_t, hidden_t, grad_t, grad_rows, pool_acc,
    gw, rw, allw, gh, rh, allh, piece_w, piece_h, learned, outgoing, arrived, small, wide,
    next_w, sends, recvs,
):
    role = lax.axis_index("role")
    me = lax.axis_index("shard")
    barrier = pltpu.get_barrier_semaphore()

    def send_all(lo, source_of, target, sem_out, sem_in):
        def body(step, carry):
            to = lax.rem(me + step, SHARDS)
            pltpu.make_async_remote_copy(
                source_of(to), target, sem_out, sem_in, (1, to), MESH
            ).start()
            return carry

        lax.fori_loop(lo, SHARDS, body, 0)

    def drain(ref, sem):
        pltpu.make_async_copy(ref, ref, sem).wait()

    @pl.when(role == 1)
    def _():
        def greet(step, carry):
            pl.semaphore_signal(barrier, inc=1, device_id=(0, step), device_id_type=MESH)

            @pl.when(step != me)
            def _():
                pl.semaphore_signal(barrier, inc=1, device_id=(1, step), device_id_type=MESH)

            return carry

        lax.fori_loop(0, SHARDS, greet, 0)

    @pl.when(role == 0)
    def _():
        pl.semaphore_signal(barrier, inc=1, device_id=(1, me), device_id_type=MESH)
        eye = identity()
        table_t[:, :HOT] = dot(eye, hot[...], NT).astype(BF)
        table_t[:, HOT:] = dot(eye, cold[...], NT).astype(BF)

        def pool_slot(slot, carry):
            own, mult = slot_rows(ids, slot)
            lanes = part(slot, N)

            def build(block, carry):
                counts[part(block, SPAN), lanes] = count_block(own, mult, block)
                return carry

            lax.fori_loop(0, TABLE // SPAN, build, 0)
            pooled_t[part(slot, E), :] = dot(table_t[...], counts[:, lanes]).astype(BF)
            return carry

        lax.fori_loop(0, SLOTS, pool_slot, 0)
        first = lax.broadcasted_iota(jnp.int32, (16, N), 0) == 0
        ones = first.astype(F32).astype(BF)

        def forward(chunk, logit):
            cols = part(chunk, 256)
            pre = dot(weight[:, cols], pooled_t[...], TN) + dot(bias[:, cols], ones, TN)
            pre_t[cols, :] = pre
            hidden = (pre * sigmoid(pre)).astype(BF)
            hidden_t[cols, :] = hidden
            return logit + dot(wout[:, cols], hidden)

        logit = lax.fori_loop(0, H // 256, forward, jnp.zeros((16, N), F32))
        scores[...] = logit[0:1]
        slope = jnp.where(first, sigmoid(logit) - labels[...], 0.0).astype(BF)

        def backward(chunk, carry):
            cols = part(chunk, 256)
            pre = pre_t[cols, :]
            gate = sigmoid(pre)
            grad = (dot(wout[:, cols], slope, TN) * (gate * (1.0 + pre * (1.0 - gate)))).astype(BF)
            grad_t[cols, :] = grad
            wide[0:16, cols] = dot(ones, grad, NT)
            wide[16:32, cols] = dot(slope, hidden_t[cols, :], NT)
            return carry

        lax.fori_loop(0, H // 256, backward, 0)
        pl.semaphore_wait(barrier, SHARDS)

        def dense(step, carry):
            chunk = lax.rem(step + me // 16, 4)
            rows = dot(pooled_t[part(chunk, 256), :], grad_t[...], NT).astype(BF)
            gw[part(chunk, 16)] = rows.reshape(16, PIECE, H)

            def send(step, carry):
                to = chunk * 16 + lax.rem(me + step, 16)
                pltpu.make_async_remote_copy(
                    gw.at[to], rw.at[me], sends.at[0], recvs.at[0], (1, to), MESH
                ).start()
                return carry

            lax.fori_loop(0, 16, send, 0)
            return carry

        lax.fori_loop(0, 4, dense, 0)

        def rows_grad(slot, carry):
            grad_rows[:, part(slot, N)] = dot(weight[part(slot, E), :], grad_t[...]).astype(BF)
            return carry

        lax.fori_loop(0, SLOTS, rows_grad, 0)
        for row in range(8):
            small[row : row + 1, :] = wide[0:1, row * E : (row + 1) * E]
            small[row + 8 : row + 9, :] = wide[16:17, row * E : (row + 1) * E]
        small_piece = jnp.broadcast_to(small[...].astype(BF)[None], (16, PIECE, E))

        def hot_grad(block, carry):
            rows = dot(counts[part(block, SPAN), :], grad_rows[...], NT).astype(BF)
            gh[part(block, 16), 0:PIECE, :] = rows.reshape(16, PIECE, E)
            gh[part(block, 16), PIECE : 2 * PIECE, :] = small_piece
            return carry

        lax.fori_loop(0, HOT // SPAN, hot_grad, 0)
        send_all(0, lambda to: gh.at[to], rh.at[me], sends.at[1], recvs.at[1])

        def cold_grad(block, carry):
            grad = dot(counts[pl.ds(pl.multiple_of(HOT + block * SPAN, SPAN), SPAN), :], grad_rows[...], NT)
            rows = part(block, SPAN)
            fresh = step_rows(cold[rows, :], grad)
            cold_out[rows, :] = fresh.astype(BF)
            marked = [
                jnp.where(pushed[block * (SPAN // BLK) + at] == 1, fresh[at * BLK : (at + 1) * BLK], unsent)
                for at in range(SPAN // BLK)
            ]
            learned[part(block, 8)] = jnp.concatenate(marked, axis=0).astype(BF).reshape(8, 32, E)
            return carry

        lax.fori_loop(0, COLD // SPAN, cold_grad, 0)

        def arrange(step, carry):
            outgoing[step] = learned[source[step]]
            return carry

        lax.fori_loop(0, SHARDS, arrange, 0)
        send_all(0, lambda to: outgoing.at[to], arrived.at[me], sends.at[2], recvs.at[2])
        drain(gw, sends.at[0])
        drain(gh, sends.at[1])
        drain(outgoing, sends.at[2])
        drain(weight_after, recvs.at[5])
        drain(hot_after, recvs.at[6])

    @pl.when(role == 1)
    def _():
        def count_slot(slot, carry):
            own, mult = slot_rows(ids, slot)
            lanes = part(slot, N)

            def build(block, carry):
                counts[part(block, SPAN), lanes] = count_block(own, mult, block)
                return carry

            return lax.fori_loop(0, TABLE // SPAN, build, carry)

        lax.fori_loop(0, SLOTS, count_slot, 0)
        pl.semaphore_wait(barrier, SHARDS)
        drain(rw, recvs.at[0])
        piece_w[...] = lax.fori_loop(
            0,
            SHARDS,
            lambda step, total: total + rw[step].astype(F32),
            jnp.zeros((PIECE, H), F32),
        ).astype(BF)
        send_all(1, lambda to: piece_w, allw.at[me], sends.at[0], recvs.at[3])
        allw[me] = piece_w[...]
        drain(rh, recvs.at[1])
        total = lax.fori_loop(
            0,
            SHARDS,
            lambda step, total: total + rh[step].astype(F32),
            jnp.zeros((2 * PIECE, E), F32),
        )
        piece_h[...] = step_rows(hot[part(me, PIECE), :], total[:PIECE]).astype(BF)
        send_all(1, lambda to: piece_h, allh.at[me], sends.at[1], recvs.at[4])
        allh[me] = piece_h[...]
        hot_after[...] = piece_h[...]
        sums = total[PIECE:]
        bias_sum, out_sum = sums[:8], sums[8:]
        bias_scale = 0.5 / jnp.sqrt(jnp.mean(bias_sum * bias_sum, keepdims=True) + epsilon)
        out_scale = (1.0 / math.sqrt(H)) / jnp.sqrt(jnp.mean(out_sum * out_sum, keepdims=True) + epsilon)
        small[0:8, :] = bias_sum * bias_scale
        small[8:16, :] = out_sum * out_scale
        wide[...] = jnp.zeros(wide.shape, F32)
        for row in range(8):
            wide[0:1, row * E : (row + 1) * E] = small[row : row + 1, :]
            wide[16:17, row * E : (row + 1) * E] = small[row + 8 : row + 9, :]
        bias_next = (bias[...].astype(F32) - wide[0:16, :]).astype(BF)
        out_next = (wout[...].astype(F32) - wide[16:32, :]).astype(BF)
        small16 = bias_next, out_next
        wide[0:16, :] = small16[0].astype(F32)
        wide[16:32, :] = small16[1].astype(F32)

        drain(arrived, recvs.at[2])
        eye = identity()

        def merge(block, carry):
            rows = part(block, SPAN)
            came = arrived[part(block, 8)].reshape(SPAN, E)
            fresh = jnp.where(came < unsent * 0.5, came, cold[rows, :])
            cold_out[rows, :] = fresh
            table_t[:, pl.ds(pl.multiple_of(HOT + block * SPAN, SPAN), SPAN)] = dot(eye, fresh, NT).astype(BF)
            return carry

        lax.fori_loop(0, COLD // SPAN, merge, 0)

        def pool_cold(slot, carry):
            pool_acc[part(slot, E), :] = dot(table_t[:, HOT:], counts[HOT:, part(slot, N)])
            return carry

        lax.fori_loop(0, SLOTS, pool_cold, 0)
        drain(allh.at[pl.ds(0, SHARDS - 1)], recvs.at[4])
        table_t[:, :HOT] = dot(eye, allh[...].reshape(HOT, E), NT).astype(BF)

        def pool_hot(slot, carry):
            rows = part(slot, E)
            pooled_t[rows, :] = (
                pool_acc[rows, :] + dot(table_t[:, :HOT], counts[:HOT, part(slot, N)])
            ).astype(BF)
            return carry

        lax.fori_loop(0, SLOTS, pool_hot, 0)
        drain(allw.at[pl.ds(0, SHARDS - 1)], recvs.at[3])

        def squares(step, total):
            value = allw[step].astype(F32)
            return total + value * value

        total = lax.fori_loop(0, SHARDS, squares, jnp.zeros((PIECE, H), F32))
        scale = (1.0 / math.sqrt(H)) / jnp.sqrt(jnp.sum(total, keepdims=True) / (H * H) + epsilon)

        def update(step, carry):
            rows = part(step, PIECE)
            next_w[rows, :] = (
                weight[rows, :].astype(F32) - allw[step].astype(F32) * scale
            ).astype(BF)
            return carry

        lax.fori_loop(0, SHARDS, update, 0)
        weight_after[...] = next_w[part(me, PIECE), :]
        piece_w2 = next_w.at[part(me, PIECE)]
        drain(allw.at[pl.ds(0, SHARDS - 1)], sends.at[0])
        drain(allh.at[pl.ds(0, SHARDS - 1)], sends.at[1])
        final_w = pltpu.make_async_remote_copy(
            piece_w2, weight_after, sends.at[2], recvs.at[5], (0, me), MESH
        )
        final_h = pltpu.make_async_remote_copy(
            piece_h, hot_after, sends.at[3], recvs.at[6], (0, me), MESH
        )
        final_w.start()
        final_h.start()
        ones = (lax.broadcasted_iota(jnp.int32, (16, N), 0) == 0).astype(F32).astype(BF)

        def score(chunk, logit):
            cols = part(chunk, 256)
            pre = dot(next_w[:, cols], pooled_t[...], TN) + dot(wide[0:16, cols].astype(BF), ones, TN)
            hidden = (pre * sigmoid(pre)).astype(BF)
            return logit + dot(wide[16:32, cols].astype(BF), hidden)

        scores[...] = lax.fori_loop(0, H // 256, score, jnp.zeros((16, N), F32))[0:1]
        final_w.wait_send()
        final_h.wait_send()


def run_round(ids, labels, hot, cold, weight, bias, wout, source, pushed):
    vmem = pl.BlockSpec(memory_space=pltpu.VMEM)
    smem = pl.BlockSpec(memory_space=pltpu.SMEM)
    return pl.pallas_call(
        round_kernel,
        out_shape=(
            jax.ShapeDtypeStruct((1, N), F32),
            jax.ShapeDtypeStruct((COLD, E), BF),
            jax.ShapeDtypeStruct((PIECE, E), BF),
            jax.ShapeDtypeStruct((PIECE, H), BF),
        ),
        in_specs=[vmem] * 7 + [smem] * 2,
        out_specs=(vmem,) * 4,
        scratch_shapes=[
            pltpu.VMEM((TABLE, SLOTS * N), BF),
            pltpu.VMEM((E, TABLE), BF),
            pltpu.VMEM((H, N), BF),
            pltpu.VMEM((H, N), F32),
            pltpu.VMEM((H, N), BF),
            pltpu.VMEM((H, N), BF),
            pltpu.VMEM((E, SLOTS * N), BF),
            pltpu.VMEM((H, N), F32),
            pltpu.VMEM((SHARDS, PIECE, H), BF),
            pltpu.VMEM((SHARDS, PIECE, H), BF),
            pltpu.VMEM((SHARDS, PIECE, H), BF),
            pltpu.VMEM((SHARDS, 2 * PIECE, E), BF),
            pltpu.VMEM((SHARDS, 2 * PIECE, E), BF),
            pltpu.VMEM((SHARDS, PIECE, E), BF),
            pltpu.VMEM((PIECE, H), BF),
            pltpu.VMEM((PIECE, E), BF),
            pltpu.VMEM((SHARDS, 32, E), BF),
            pltpu.VMEM((SHARDS, 32, E), BF),
            pltpu.VMEM((SHARDS, 32, E), BF),
            pltpu.VMEM((16, E), F32),
            pltpu.VMEM((32, H), F32),
            pltpu.VMEM((H, H), BF),
            pltpu.SemaphoreType.DMA((4,)),
            pltpu.SemaphoreType.DMA((7,)),
        ],
        compiler_params=pltpu.CompilerParams(
            collective_id=0, has_side_effects=True, vmem_limit_bytes=58 << 20
        ),
        name="round",
    )(ids, labels, hot, cold, weight, bias, wout, source, pushed)


def on_device(
    feature_ids, labels, cold_rows, hot_rows, block_owner, pushed, weight_in, bias_in, weight_out
):
    owner_ids = lax.broadcasted_iota(jnp.int32, (SHARDS, SHARDS), 1)
    group_ids = lax.broadcasted_iota(jnp.int32, (SHARDS, SHARDS), 0)
    owner_match = (block_owner[0][:, None] == owner_ids).astype(jnp.int32)
    source = jnp.sum(owner_match * group_ids, axis=0)
    scores, cold_out, hot_after, weight_after = run_round(
        feature_ids[0],
        labels[None],
        hot_rows,
        cold_rows[0],
        weight_in,
        jnp.pad(bias_in[None], ((0, 15), (0, 0))),
        jnp.pad(weight_out[None], ((0, 15), (0, 0))),
        source,
        pushed,
    )
    return (scores, cold_out[None], hot_after, weight_after)


def solution(mesh):
    in_specs = (
        P("role", None, None, "shard"),
        P("shard"),
        P("role", "shard", None),
        P(),
        P("shard", None),
        P("shard"),
        P(),
        P(),
        P(),
    )
    out_specs = (P("role", "shard"), P("role", "shard", None), P("shard", None), P("shard", None))
    return jax.shard_map(
        on_device, mesh=mesh, in_specs=in_specs, out_specs=out_specs, check_vma=False
    )
```

profile of v0, /device:TPU:17, one launch (start us, length us, event | category | flops | bytes accessed | tf_op | source)
XLA Modules:
  0.0 85.3 jit_solution(12195813406680799617)
XLA Ops:
  0.6 1.3 %select_reduce_fusion.source = s32[64]{0:T(128)} fusion(s32[64]{0:T(128)} %bitcast.9), kind=kLoop, calls=%fused_computation | loop fusion | flops 12224 | bytes 512 | tf_op jit(solution)/shard_map/reduce_sum | solution.py:395
  1.9 0.7 broadcast_in_dim.13
  2.6 0.7 broadcast_in_dim.14
  3.3 0.6 pad.8.wout
  3.9 0.6 pad.7.bias
  4.5 75.1 %round.1 = (f32[1,512]{1,0:T(1,128)}, bf16[2048,128]{1,0:T(8,128)(2,1)}, bf16[16,128]{1,0:T(8,128)(2,1)}, bf16[16,1024]{1,0:T(8,128)(2,1)}) custom-call(s32[8,4,512]{2,1,0:T(4,128)} %bitcast.7, f32[1,512]{1,0:T(1,128)} %bitcast.8, bf16[1024,128]{1,0:T(8,128)(2,1)} %hot.1, bf16[2048,128]{1,0:T(8,128)(2,1)} %bitcast.6, bf16[1024,1024]{1,0:T(8,128)(2,1)} %weight.1, ...), custom_call_target="tpu_custom_call" | custom-call | tf_op jit(solution)/shard_map/round/pallas_call | solution.py:346
  79.6 1.2 %copy.17 = f32[1,512]{1,0:T(1,128)} copy(f32[1,512]{1,0:T(1,128)} %get-tuple-element.16) | data formatting | bytes 4096
  80.8 1.9 %copy.18 = bf16[1,2048,128]{2,1,0:T(8,128)(2,1)} copy(bf16[1,2048,128]{2,1,0:T(8,128)(2,1)} %bitcast.5) | data formatting | bytes 1048576
  82.7 1.3 %copy.19 = bf16[16,128]{1,0:T(8,128)(2,1)} copy(bf16[16,128]{1,0:T(8,128)(2,1)} %get-tuple-element.18) | data formatting | bytes 8192
  84.0 1.4 %copy.20 = bf16[16,1024]{1,0:T(8,128)(2,1)} copy(bf16[16,1024]{1,0:T(8,128)(2,1)} %get-tuple-element.19) | data formatting | bytes 65536
where the time goes:
time: 85.7 us; the launch traced here: 85.3 us
  Pallas kernels  75.1 us (88%)
  local copies, waits for them, and re-layouts  8.37 us (10%)
  other arithmetic  1.26 us (1%)
    pallas_call x1, Pallas kernels, run_round(): pl.pallas_call(round_kernel, out_shape=(jax.ShapeDtypeStruct((1, N), F32)...  75.1 us
    unnamed x4, local copies, waits for them, and re-layouts  5.76 us

commit v1 on v0

--- a/solution.py
+++ b/solution.py
@@ -73,15 +73,18 @@
 
 
 def round_kernel(
-    ids, labels, hot, cold, weight, bias, wout, source, pushed,
+    ids, labels, hot, cold, weight, bias_in, weight_out, owner, pushed,
     scores, cold_out, hot_after, weight_after,
     counts, table_t, pooled_t, pre_t, hidden_t, grad_t, grad_rows, pool_acc,
     gw, rw, allw, gh, rh, allh, piece_w, piece_h, learned, outgoing, arrived, small, wide,
-    next_w, sends, recvs,
+    next_w, bias, wout, source_rows, source, sends, recvs, local,
 ):
     role = lax.axis_index("role")
     me = lax.axis_index("shard")
     barrier = pltpu.get_barrier_semaphore()
+    top = lax.broadcasted_iota(jnp.int32, (16, H), 0) == 0
+    bias[...] = jnp.where(top, bias_in[...].reshape(1, H).astype(F32), 0.0).astype(BF)
+    wout[...] = jnp.where(top, weight_out[...].reshape(1, H).astype(F32), 0.0).astype(BF)
 
     def send_all(lo, source_of, target, sem_out, sem_in):
         def body(step, carry):
@@ -112,6 +115,13 @@
     @pl.when(role == 0)
     def _():
         pl.semaphore_signal(barrier, inc=1, device_id=(1, me), device_id_type=MESH)
+        groups = lax.broadcasted_iota(jnp.int32, (SHARDS, SHARDS), 1)
+        owners = lax.broadcasted_iota(jnp.int32, (SHARDS, SHARDS), 0)
+        found = jnp.where(owner[...] == owners, groups, 0)
+        spot = jnp.clip(jnp.sum(found, axis=1, keepdims=True), 0, SHARDS - 1)
+        source_rows[...] = jnp.broadcast_to(spot, (SHARDS, E))
+        fetch = pltpu.make_async_copy(source_rows, source, local.at[0])
+        fetch.start()
         eye = identity()
         table_t[:, :HOT] = dot(eye, hot[...], NT).astype(BF)
         table_t[:, HOT:] = dot(eye, cold[...], NT).astype(BF)
@@ -142,7 +152,7 @@
 
         logit = lax.fori_loop(0, H // 256, forward, jnp.zeros((16, N), F32))
         scores[...] = logit[0:1]
-        slope = jnp.where(first, sigmoid(logit) - labels[...], 0.0).astype(BF)
+        slope = jnp.where(first, sigmoid(logit) - labels[...].reshape(1, N), 0.0).astype(BF)
 
         def backward(chunk, carry):
             cols = part(chunk, 256)
@@ -207,8 +217,10 @@
 
         lax.fori_loop(0, COLD // SPAN, cold_grad, 0)
 
+        fetch.wait()
+
         def arrange(step, carry):
-            outgoing[step] = learned[source[step]]
+            outgoing[step] = learned[jnp.clip(source[step, 0], 0, SHARDS - 1)]
             return carry
 
         lax.fori_loop(0, SHARDS, arrange, 0)
@@ -340,7 +352,7 @@
         final_h.wait_send()
 
 
-def run_round(ids, labels, hot, cold, weight, bias, wout, source, pushed):
+def run_round(ids, labels, hot, cold, weight, bias, wout, owner, pushed):
     vmem = pl.BlockSpec(memory_space=pltpu.VMEM)
     smem = pl.BlockSpec(memory_space=pltpu.SMEM)
     return pl.pallas_call(
@@ -351,7 +363,7 @@
             jax.ShapeDtypeStruct((PIECE, E), BF),
             jax.ShapeDtypeStruct((PIECE, H), BF),
         ),
-        in_specs=[vmem] * 7 + [smem] * 2,
+        in_specs=[vmem] * 8 + [smem],
         out_specs=(vmem,) * 4,
         scratch_shapes=[
             pltpu.VMEM((TABLE, SLOTS * N), BF),
@@ -376,33 +388,58 @@
             pltpu.VMEM((16, E), F32),
             pltpu.VMEM((32, H), F32),
             pltpu.VMEM((H, H), BF),
+            pltpu.VMEM((16, H), BF),
+            pltpu.VMEM((16, H), BF),
+            pltpu.VMEM((SHARDS, E), jnp.int32),
+            pltpu.SMEM((SHARDS, E), jnp.int32),
             pltpu.SemaphoreType.DMA((4,)),
             pltpu.SemaphoreType.DMA((7,)),
+            pltpu.SemaphoreType.DMA((1,)),
         ],
         compiler_params=pltpu.CompilerParams(
             collective_id=0, has_side_effects=True, vmem_limit_bytes=58 << 20
         ),
         name="round",
-    )(ids, labels, hot, cold, weight, bias, wout, source, pushed)
+    )(ids, labels, hot, cold, weight, bias, wout, owner, pushed)
+
+
+def hand_over_kernel(*refs):
+    count = len(refs) // 2
+    copies = [
+        pltpu.make_async_copy(refs[at], refs[count + at], refs[-1].at[at]) for at in range(count)
+    ]
+    for copy in copies:
+        copy.start()
+    for copy in copies:
+        copy.wait()
+
+
+def hand_over(arrays):
+    return pl.pallas_call(
+        hand_over_kernel,
+        out_shape=tuple(jax.ShapeDtypeStruct(array.shape, array.dtype) for array in arrays),
+        in_specs=[pl.BlockSpec(memory_space=pl.ANY)] * len(arrays),
+        out_specs=(pl.BlockSpec(memory_space=pl.ANY),) * len(arrays),
+        scratch_shapes=[pltpu.SemaphoreType.DMA((len(arrays),))],
+        name="hand_over",
+    )(*arrays)
 
 
 def on_device(
     feature_ids, labels, cold_rows, hot_rows, block_owner, pushed, weight_in, bias_in, weight_out
 ):
-    owner_ids = lax.broadcasted_iota(jnp.int32, (SHARDS, SHARDS), 1)
-    group_ids = lax.broadcasted_iota(jnp.int32, (SHARDS, SHARDS), 0)
-    owner_match = (block_owner[0][:, None] == owner_ids).astype(jnp.int32)
-    source = jnp.sum(owner_match * group_ids, axis=0)
-    scores, cold_out, hot_after, weight_after = run_round(
-        feature_ids[0],
-        labels[None],
-        hot_rows,
-        cold_rows[0],
-        weight_in,
-        jnp.pad(bias_in[None], ((0, 15), (0, 0))),
-        jnp.pad(weight_out[None], ((0, 15), (0, 0))),
-        source,
-        pushed,
+    scores, cold_out, hot_after, weight_after = hand_over(
+        run_round(
+            feature_ids[0],
+            labels,
+            hot_rows,
+            cold_rows[0],
+            weight_in,
+            bias_in,
+            weight_out,
+            block_owner,
+            pushed,
+        )
     )
     return (scores, cold_out[None], hot_after, weight_after)
 

time: 85.7 us -> 94.1 us (1.098)
  the two profiles are of different devices: /device:TPU:17 before, /device:TPU:1 now
where the time goes in v1:
time: 94.1 us; the launch traced here: 92.9 us
  Pallas kernels  92.3 us (98%)
    pallas_call x1, Pallas kernels, run_round(): pl.pallas_call(round_kernel, out_shape=(jax.ShapeDtypeStruct((1, N), F32)...  74.1 us
    pallas_call x1, Pallas kernels, hand_over(): pl.pallas_call(hand_over_kernel, out_shape=tuple((jax.ShapeDtypeStruct(ar...  18.2 us

profile of v1, /device:TPU:1, one launch (start us, length us, event | category | flops | bytes accessed | tf_op | source)
XLA Modules:
  0.0 92.9 jit_solution(5717003682144768159)
XLA Ops:
  0.6 74.1 %round.1 = (f32[1,512]{1,0:T(1,128)}, bf16[2048,128]{1,0:T(8,128)(2,1)}, bf16[16,128]{1,0:T(8,128)(2,1)}, bf16[16,1024]{1,0:T(8,128)(2,1)}) custom-call(s32[8,4,512]{2,1,0:T(4,128)} %bitcast.4, f32[512]{0:T(512)} %labels.1, bf16[1024,128]{1,0:T(8,128)(2,1)} %hot.1, bf16[2048,128]{1,0:T(8,128)(2,1)} %bitcast.3, bf16[1024,1024]{1,0:T(8,128)(2,1)} %weight.1, ...), custom_call_target="tpu_custom_call" | custom-call | tf_op jit(solution)/shard_map/round/pallas_call | solution.py:358
  74.7 18.2 %hand_over.1 = (f32[1,512]{1,0:T(1,128)}, bf16[2048,128]{1,0:T(8,128)(2,1)}, bf16[16,128]{1,0:T(8,128)(2,1)}, bf16[16,1024]{1,0:T(8,128)(2,1)}) custom-call(f32[1,512]{1,0:T(1,128)} %get-tuple-element.12.refs_0_, bf16[2048,128]{1,0:T(8,128)(2,1)} %get-tuple-element.13.refs_1_, bf16[16,128]{1,0:T(8,128)(2,1)} %get-tuple-element.14.refs_2_, ...), custom_call_target="tpu_custom_call" | custom-call | tf_op jit(solution)/shard_map/hand_over/pallas_call | solution.py:418

commit v2 on v1

--- a/solution.py
+++ b/solution.py
@@ -419,7 +419,7 @@
         hand_over_kernel,
         out_shape=tuple(jax.ShapeDtypeStruct(array.shape, array.dtype) for array in arrays),
         in_specs=[pl.BlockSpec(memory_space=pl.ANY)] * len(arrays),
-        out_specs=(pl.BlockSpec(memory_space=pl.ANY),) * len(arrays),
+        out_specs=(pl.BlockSpec(memory_space=pltpu.VMEM),) * len(arrays),
         scratch_shapes=[pltpu.SemaphoreType.DMA((len(arrays),))],
         name="hand_over",
     )(*arrays)

time: 94.1 us -> 77.8 us (0.83)
  Pallas kernels: 92.3 us -> 76 us
    pallas_call x1, Pallas kernels: 18.2 us -> 1.88 us  [hand_over(): pl.pallas_call(hand_over_kernel, out_shape=tuple((jax.ShapeDtypeStruct(ar...]
where the time goes in v2:
time: 77.8 us; the launch traced here: 76.6 us
  Pallas kernels  76 us (98%)
    pallas_call x1, Pallas kernels, run_round(): pl.pallas_call(round_kernel, out_shape=(jax.ShapeDtypeStruct((1, N), F32)...  74.1 us
    pallas_call x1, Pallas kernels, hand_over(): pl.pallas_call(hand_over_kernel, out_shape=tuple((jax.ShapeDtypeStruct(ar...  1.88 us

profile of v2, /device:TPU:1, one launch (start us, length us, event | category | flops | bytes accessed | tf_op | source)
XLA Modules:
  0.0 76.6 jit_solution(13842336250099533345)
XLA Ops:
  0.6 74.1 %round.1 = (f32[1,512]{1,0:T(1,128)}, bf16[2048,128]{1,0:T(8,128)(2,1)}, bf16[16,128]{1,0:T(8,128)(2,1)}, bf16[16,1024]{1,0:T(8,128)(2,1)}) custom-call(s32[8,4,512]{2,1,0:T(4,128)} %bitcast.4, f32[512]{0:T(512)} %labels.1, bf16[1024,128]{1,0:T(8,128)(2,1)} %hot.1, bf16[2048,128]{1,0:T(8,128)(2,1)} %bitcast.3, bf16[1024,1024]{1,0:T(8,128)(2,1)} %weight.1, ...), custom_call_target="tpu_custom_call" | custom-call | tf_op jit(solution)/shard_map/round/pallas_call | solution.py:358
  74.7 1.9 %hand_over.1 = (f32[1,512]{1,0:T(1,128)}, bf16[2048,128]{1,0:T(8,128)(2,1)}, bf16[16,128]{1,0:T(8,128)(2,1)}, bf16[16,1024]{1,0:T(8,128)(2,1)}) custom-call(f32[1,512]{1,0:T(1,128)} %get-tuple-element.12.refs_0_, bf16[2048,128]{1,0:T(8,128)(2,1)} %get-tuple-element.13.refs_1_, bf16[16,128]{1,0:T(8,128)(2,1)} %get-tuple-element.14.refs_2_, ...), custom_call_target="tpu_custom_call" | custom-call | tf_op jit(solution)/shard_map/hand_over/pallas_call | solution.py:418

commit v3 on v2

--- a/solution.py
+++ b/solution.py
@@ -29,6 +29,7 @@
 PIECE = H // SHARDS
 BLK = 8
 SPAN = 256
+CHUNKS = ((0, 384), (384, 384), (768, 256))
 
 
 def dot(lhs, rhs, dims=NN):
@@ -72,15 +73,41 @@
     return acc
 
 
+def line_of(ref, axis, index, cols):
+    at = [slice(None)] * 3
+    at[axis] = index
+    return ref.at[(*at, slice(None), cols)]
+
+
+def shard_of(coords):
+    return coords[0] * 16 + coords[1] * 4 + coords[2]
+
+
+def on_line(coords, axis, index):
+    return shard_of([index if other == axis else coords[other] for other in range(3)])
+
+
+def in_plane(coords, axis, index):
+    spots = iter((index // 4, lax.rem(index, 4)))
+    return shard_of([coords[axis] if other == axis else next(spots) for other in range(3)])
+
+
+def plane_index(coords, axis):
+    first, second = [coords[other] for other in range(3) if other != axis]
+    return first * 4 + second
+
+
 def round_kernel(
     ids, labels, hot, cold, weight, bias_in, weight_out, owner, pushed,
     scores, cold_out, hot_after, weight_after,
     counts, table_t, pooled_t, pre_t, hidden_t, grad_t, grad_rows, pool_acc,
-    gw, rw, allw, gh, rh, allh, piece_w, piece_h, learned, outgoing, arrived, small, wide,
+    gw, rw0, rw1, rw2, line0, line1, line2, plane0, plane1, plane2, allw, gh, rh, allh, piece_w, piece_h, learned, outgoing, arrived, small, wide,
     next_w, bias, wout, source_rows, source, sends, recvs, local,
 ):
     role = lax.axis_index("role")
     me = lax.axis_index("shard")
+    coords = (me // 16, lax.rem(me // 4, 4), lax.rem(me, 4))
+    rw, line, plane = (rw0, rw1, rw2), (line0, line1, line2), (plane0, plane1, plane2)
     barrier = pltpu.get_barrier_semaphore()
     top = lax.broadcasted_iota(jnp.int32, (16, H), 0) == 0
     bias[...] = jnp.where(top, bias_in[...].reshape(1, H).astype(F32), 0.0).astype(BF)
@@ -167,22 +194,25 @@
         lax.fori_loop(0, H // 256, backward, 0)
         pl.semaphore_wait(barrier, SHARDS)
 
-        def dense(step, carry):
-            chunk = lax.rem(step + me // 16, 4)
-            rows = dot(pooled_t[part(chunk, 256), :], grad_t[...], NT).astype(BF)
-            gw[part(chunk, 16)] = rows.reshape(16, PIECE, H)
-
-            def send(step, carry):
-                to = chunk * 16 + lax.rem(me + step, 16)
+        for axis, (first_col, width) in enumerate(CHUNKS):
+            cols = pl.ds(first_col, width)
+
+            def dense(chunk, carry):
+                rows = dot(pooled_t[part(chunk, 256), :], grad_t[cols, :], NT).astype(BF)
+                gw[chunk, :, :, :, cols] = rows.reshape(4, 4, PIECE, width)
+                return carry
+
+            lax.fori_loop(0, 4, dense, 0)
+            for step in range(4):
+                index = lax.rem(coords[axis] + step, 4)
                 pltpu.make_async_remote_copy(
-                    gw.at[to], rw.at[me], sends.at[0], recvs.at[0], (1, to), MESH
+                    line_of(gw, axis, index, cols),
+                    rw[axis].at[coords[axis]],
+                    sends.at[0],
+                    recvs.at[axis],
+                    (1, on_line(coords, axis, index)),
+                    MESH,
                 ).start()
-                return carry
-
-            lax.fori_loop(0, 16, send, 0)
-            return carry
-
-        lax.fori_loop(0, 4, dense, 0)
 
         def rows_grad(slot, carry):
             grad_rows[:, part(slot, N)] = dot(weight[part(slot, E), :], grad_t[...]).astype(BF)
@@ -201,7 +231,7 @@
             return carry
 
         lax.fori_loop(0, HOT // SPAN, hot_grad, 0)
-        send_all(0, lambda to: gh.at[to], rh.at[me], sends.at[1], recvs.at[1])
+        send_all(0, lambda to: gh.at[to], rh.at[me], sends.at[1], recvs.at[12])
 
         def cold_grad(block, carry):
             grad = dot(counts[pl.ds(pl.multiple_of(HOT + block * SPAN, SPAN), SPAN), :], grad_rows[...], NT)
@@ -224,12 +254,12 @@
             return carry
 
         lax.fori_loop(0, SHARDS, arrange, 0)
-        send_all(0, lambda to: outgoing.at[to], arrived.at[me], sends.at[2], recvs.at[2])
+        send_all(0, lambda to: outgoing.at[to], arrived.at[me], sends.at[2], recvs.at[13])
         drain(gw, sends.at[0])
         drain(gh, sends.at[1])
         drain(outgoing, sends.at[2])
-        drain(weight_after, recvs.at[5])
-        drain(hot_after, recvs.at[6])
+        drain(weight_after, recvs.at[15])
+        drain(hot_after, recvs.at[16])
 
     @pl.when(role == 1)
     def _():
@@ -245,16 +275,58 @@
 
         lax.fori_loop(0, SLOTS, count_slot, 0)
         pl.semaphore_wait(barrier, SHARDS)
-        drain(rw, recvs.at[0])
-        piece_w[...] = lax.fori_loop(
-            0,
-            SHARDS,
-            lambda step, total: total + rw[step].astype(F32),
-            jnp.zeros((PIECE, H), F32),
-        ).astype(BF)
-        send_all(1, lambda to: piece_w, allw.at[me], sends.at[0], recvs.at[3])
-        allw[me] = piece_w[...]
-        drain(rh, recvs.at[1])
+        for axis, (first_col, width) in enumerate(CHUNKS):
+            drain(rw[axis], recvs.at[axis])
+
+            def add_line(step, carry):
+                at = (step // 4, lax.rem(step, 4))
+                total = sum(rw[axis][(source, *at)].astype(F32) for source in range(4))
+                line[axis][step] = total.astype(BF)
+                return carry
+
+            lax.fori_loop(0, 16, add_line, 0)
+            own = plane_index(coords, axis)
+
+            def send_plane(step, carry):
+                index = lax.rem(own + step, 16)
+                pltpu.make_async_remote_copy(
+                    line[axis].at[index],
+                    plane[axis].at[own],
+                    sends.at[axis],
+                    recvs.at[3 + axis],
+                    (1, in_plane(coords, axis, index)),
+                    MESH,
+                ).start()
+                return carry
+
+            lax.fori_loop(1, 16, send_plane, 0)
+            plane[axis][own] = line[axis][own]
+        for axis, (first_col, width) in enumerate(CHUNKS):
+            cols = pl.ds(first_col, width)
+            drain(plane[axis].at[pl.ds(0, 15)], recvs.at[3 + axis])
+            total = lax.fori_loop(
+                0,
+                16,
+                lambda step, total: total + plane[axis][step].astype(F32),
+                jnp.zeros((PIECE, width), F32),
+            ).astype(BF)
+            piece_w[:, cols] = total
+            allw[(*coords, slice(None), cols)] = total
+            own = plane_index(coords, axis)
+
+            def spread_plane(step, carry):
+                pltpu.make_async_remote_copy(
+                    piece_w.at[:, cols],
+                    allw.at[(*coords, slice(None), cols)],
+                    sends.at[3 + axis],
+                    recvs.at[6 + axis],
+                    (1, in_plane(coords, axis, lax.rem(own + step, 16))),
+                    MESH,
+                ).start()
+                return carry
+
+            lax.fori_loop(1, 16, spread_plane, 0)
+        drain(rh, recvs.at[12])
         total = lax.fori_loop(
             0,
             SHARDS,
@@ -262,9 +334,22 @@
             jnp.zeros((2 * PIECE, E), F32),
         )
         piece_h[...] = step_rows(hot[part(me, PIECE), :], total[:PIECE]).astype(BF)
-        send_all(1, lambda to: piece_h, allh.at[me], sends.at[1], recvs.at[4])
+        send_all(1, lambda to: piece_h, allh.at[me], sends.at[9], recvs.at[14])
         allh[me] = piece_h[...]
         hot_after[...] = piece_h[...]
+        for axis, (first_col, width) in enumerate(CHUNKS):
+            cols = pl.ds(first_col, width)
+            drain(plane[axis].at[pl.ds(0, 15)], recvs.at[6 + axis])
+            for step in range(1, 4):
+                index = lax.rem(coords[axis] + step, 4)
+                pltpu.make_async_remote_copy(
+                    line_of(allw, axis, coords[axis], cols),
+                    line_of(allw, axis, coords[axis], cols),
+                    sends.at[6 + axis],
+                    recvs.at[9 + axis],
+                    (1, on_line(coords, axis, index)),
+                    MESH,
+                ).start()
         sums = total[PIECE:]
         bias_sum, out_sum = sums[:8], sums[8:]
         bias_scale = 0.5 / jnp.sqrt(jnp.mean(bias_sum * bias_sum, keepdims=True) + epsilon)
@@ -281,7 +366,7 @@
         wide[0:16, :] = small16[0].astype(F32)
         wide[16:32, :] = small16[1].astype(F32)
 
-        drain(arrived, recvs.at[2])
+        drain(arrived, recvs.at[13])
         eye = identity()
 
         def merge(block, carry):
@@ -299,7 +384,7 @@
             return carry
 
         lax.fori_loop(0, SLOTS, pool_cold, 0)
-        drain(allh.at[pl.ds(0, SHARDS - 1)], recvs.at[4])
+        drain(allh.at[pl.ds(0, SHARDS - 1)], recvs.at[14])
         table_t[:, :HOT] = dot(eye, allh[...].reshape(HOT, E), NT).astype(BF)
 
         def pool_hot(slot, carry):
@@ -310,10 +395,11 @@
             return carry
 
         lax.fori_loop(0, SLOTS, pool_hot, 0)
-        drain(allw.at[pl.ds(0, SHARDS - 1)], recvs.at[3])
+        for axis in range(3):
+            drain(rw[axis].at[pl.ds(0, 3)], recvs.at[9 + axis])
 
         def squares(step, total):
-            value = allw[step].astype(F32)
+            value = allw[step // 16, lax.rem(step // 4, 4), lax.rem(step, 4)].astype(F32)
             return total + value * value
 
         total = lax.fori_loop(0, SHARDS, squares, jnp.zeros((PIECE, H), F32))
@@ -322,20 +408,23 @@
         def update(step, carry):
             rows = part(step, PIECE)
             next_w[rows, :] = (
-                weight[rows, :].astype(F32) - allw[step].astype(F32) * scale
+                weight[rows, :].astype(F32) - allw[step // 16, lax.rem(step // 4, 4), lax.rem(step, 4)].astype(F32) * scale
             ).astype(BF)
             return carry
 
         lax.fori_loop(0, SHARDS, update, 0)
         weight_after[...] = next_w[part(me, PIECE), :]
         piece_w2 = next_w.at[part(me, PIECE)]
-        drain(allw.at[pl.ds(0, SHARDS - 1)], sends.at[0])
-        drain(allh.at[pl.ds(0, SHARDS - 1)], sends.at[1])
+        for axis in range(3):
+            drain(plane[axis].at[pl.ds(0, 15)], sends.at[axis])
+            drain(plane[axis].at[pl.ds(0, 15)], sends.at[3 + axis])
+            drain(rw[axis].at[pl.ds(0, 3)], sends.at[6 + axis])
+        drain(allh.at[pl.ds(0, SHARDS - 1)], sends.at[9])
         final_w = pltpu.make_async_remote_copy(
-            piece_w2, weight_after, sends.at[2], recvs.at[5], (0, me), MESH
+            piece_w2, weight_after, sends.at[10], recvs.at[15], (0, me), MESH
         )
         final_h = pltpu.make_async_remote_copy(
-            piece_h, hot_after, sends.at[3], recvs.at[6], (0, me), MESH
+            piece_h, hot_after, sends.at[11], recvs.at[16], (0, me), MESH
         )
         final_w.start()
         final_h.start()
@@ -374,9 +463,11 @@
             pltpu.VMEM((H, N), BF),
             pltpu.VMEM((E, SLOTS * N), BF),
             pltpu.VMEM((H, N), F32),
-            pltpu.VMEM((SHARDS, PIECE, H), BF),
-            pltpu.VMEM((SHARDS, PIECE, H), BF),
-            pltpu.VMEM((SHARDS, PIECE, H), BF),
+            pltpu.VMEM((4, 4, 4, PIECE, H), BF),
+            *[pltpu.VMEM((4, 4, 4, PIECE, width), BF) for _, width in CHUNKS],
+            *[pltpu.VMEM((16, PIECE, width), BF) for _, width in CHUNKS],
+            *[pltpu.VMEM((16, PIECE, width), BF) for _, width in CHUNKS],
+            pltpu.VMEM((4, 4, 4, PIECE, H), BF),
             pltpu.VMEM((SHARDS, 2 * PIECE, E), BF),
             pltpu.VMEM((SHARDS, 2 * PIECE, E), BF),
             pltpu.VMEM((SHARDS, PIECE, E), BF),
@@ -392,8 +483,8 @@
             pltpu.VMEM((16, H), BF),
             pltpu.VMEM((SHARDS, E), jnp.int32),
             pltpu.SMEM((SHARDS, E), jnp.int32),
-            pltpu.SemaphoreType.DMA((4,)),
-            pltpu.SemaphoreType.DMA((7,)),
+            pltpu.SemaphoreType.DMA((12,)),
+            pltpu.SemaphoreType.DMA((17,)),
             pltpu.SemaphoreType.DMA((1,)),
         ],
         compiler_params=pltpu.CompilerParams(

time: 77.8 us -> 70.9 us (0.911); the launches traced: 76.6 us -> 70.7 us
  Pallas kernels: 76 us -> 70 us
    pallas_call x1, Pallas kernels: 74.1 us -> 68.2 us  [run_round(): pl.pallas_call(round_kernel, out_shape=(jax.ShapeDtypeStruct((1, N), F32)...]
where the time goes in v3:
time: 70.9 us; the launch traced here: 70.7 us
  Pallas kernels  70 us (99%)
    pallas_call x1, Pallas kernels, run_round(): pl.pallas_call(round_kernel, out_shape=(jax.ShapeDtypeStruct((1, N), F32)...  68.2 us
    pallas_call x1, Pallas kernels, hand_over(): pl.pallas_call(hand_over_kernel, out_shape=tuple((jax.ShapeDtypeStruct(ar...  1.88 us

profile of v3, /device:TPU:1, one launch (start us, length us, event | category | flops | bytes accessed | tf_op | source)
XLA Modules:
  0.0 70.7 jit_solution(8590869435552525261)
XLA Ops:
  0.6 68.2 %round.1 = (f32[1,512]{1,0:T(1,128)}, bf16[2048,128]{1,0:T(8,128)(2,1)}, bf16[16,128]{1,0:T(8,128)(2,1)}, bf16[16,1024]{1,0:T(8,128)(2,1)}) custom-call(s32[8,4,512]{2,1,0:T(4,128)} %bitcast.4, f32[512]{0:T(512)} %labels.1, bf16[1024,128]{1,0:T(8,128)(2,1)} %hot.1, bf16[2048,128]{1,0:T(8,128)(2,1)} %bitcast.3, bf16[1024,1024]{1,0:T(8,128)(2,1)} %weight.1, ...), custom_call_target="tpu_custom_call" | custom-call | tf_op jit(solution)/shard_map/round/pallas_call | solution.py:447
  68.8 1.9 %hand_over.1 = (f32[1,512]{1,0:T(1,128)}, bf16[2048,128]{1,0:T(8,128)(2,1)}, bf16[16,128]{1,0:T(8,128)(2,1)}, bf16[16,1024]{1,0:T(8,128)(2,1)}) custom-call(f32[1,512]{1,0:T(1,128)} %get-tuple-element.12.refs_0_, bf16[2048,128]{1,0:T(8,128)(2,1)} %get-tuple-element.13.refs_1_, bf16[16,128]{1,0:T(8,128)(2,1)} %get-tuple-element.14.refs_2_, ...), custom_call_target="tpu_custom_call" | custom-call | tf_op jit(solution)/shard_map/hand_over/pallas_call | solution.py:509

commit v4 on v3

--- a/solution.py
+++ b/solution.py
@@ -29,6 +29,7 @@
 PIECE = H // SHARDS
 BLK = 8
 SPAN = 256
+STEP = 512
 CHUNKS = ((0, 384), (384, 384), (768, 256))
 
 
@@ -41,8 +42,8 @@
 
 
 def step_rows(old_rows, grad_rows):
-    scale_rows = jnp.sqrt(jnp.mean(grad_rows * grad_rows, axis=-1, keepdims=True) + epsilon)
-    return old_rows.astype(F32) - row_rate * grad_rows / scale_rows
+    scale_rows = row_rate * lax.rsqrt(jnp.mean(grad_rows * grad_rows, axis=-1, keepdims=True) + epsilon)
+    return old_rows.astype(F32) - grad_rows * scale_rows
 
 
 def part(index, size):
@@ -102,7 +103,7 @@
     scores, cold_out, hot_after, weight_after,
     counts, table_t, pooled_t, pre_t, hidden_t, grad_t, grad_rows, pool_acc,
     gw, rw0, rw1, rw2, line0, line1, line2, plane0, plane1, plane2, allw, gh, rh, allh, piece_w, piece_h, learned, outgoing, arrived, small, wide,
-    next_w, bias, wout, source_rows, source, sends, recvs, local,
+    bias, wout, source_rows, source, sends, recvs, local,
 ):
     role = lax.axis_index("role")
     me = lax.axis_index("shard")
@@ -153,19 +154,12 @@
         table_t[:, :HOT] = dot(eye, hot[...], NT).astype(BF)
         table_t[:, HOT:] = dot(eye, cold[...], NT).astype(BF)
 
-        def pool_slot(slot, carry):
+        for slot in range(SLOTS):
             own, mult = slot_rows(ids, slot)
-            lanes = part(slot, N)
-
-            def build(block, carry):
-                counts[part(block, SPAN), lanes] = count_block(own, mult, block)
-                return carry
-
-            lax.fori_loop(0, TABLE // SPAN, build, 0)
-            pooled_t[part(slot, E), :] = dot(table_t[...], counts[:, lanes]).astype(BF)
-            return carry
-
-        lax.fori_loop(0, SLOTS, pool_slot, 0)
+            lanes = slice(slot * N, (slot + 1) * N)
+            for block in range(TABLE // SPAN):
+                counts[block * SPAN : (block + 1) * SPAN, lanes] = count_block(own, mult, block)
+            pooled_t[slot * E : (slot + 1) * E, :] = dot(table_t[...], counts[:, lanes]).astype(BF)
         first = lax.broadcasted_iota(jnp.int32, (16, N), 0) == 0
         ones = first.astype(F32).astype(BF)
 
@@ -224,29 +218,26 @@
             small[row + 8 : row + 9, :] = wide[16:17, row * E : (row + 1) * E]
         small_piece = jnp.broadcast_to(small[...].astype(BF)[None], (16, PIECE, E))
 
-        def hot_grad(block, carry):
-            rows = dot(counts[part(block, SPAN), :], grad_rows[...], NT).astype(BF)
-            gh[part(block, 16), 0:PIECE, :] = rows.reshape(16, PIECE, E)
-            gh[part(block, 16), PIECE : 2 * PIECE, :] = small_piece
-            return carry
-
-        lax.fori_loop(0, HOT // SPAN, hot_grad, 0)
+        for block in range(HOT // STEP):
+            rows = dot(counts[block * STEP : (block + 1) * STEP, :], grad_rows[...], NT).astype(BF)
+            at = pl.ds(block * (STEP // PIECE), STEP // PIECE)
+            gh[at, 0:PIECE, :] = rows.reshape(STEP // PIECE, PIECE, E)
+        for block in range(4):
+            gh[block * 16 : block * 16 + 16, PIECE : 2 * PIECE, :] = small_piece
         send_all(0, lambda to: gh.at[to], rh.at[me], sends.at[1], recvs.at[12])
-
-        def cold_grad(block, carry):
-            grad = dot(counts[pl.ds(pl.multiple_of(HOT + block * SPAN, SPAN), SPAN), :], grad_rows[...], NT)
-            rows = part(block, SPAN)
+        for block in range(COLD // STEP):
+            rows = pl.ds(block * STEP, STEP)
+            grad = dot(counts[pl.ds(HOT + block * STEP, STEP), :], grad_rows[...], NT)
             fresh = step_rows(cold[rows, :], grad)
             cold_out[rows, :] = fresh.astype(BF)
             marked = [
-                jnp.where(pushed[block * (SPAN // BLK) + at] == 1, fresh[at * BLK : (at + 1) * BLK], unsent)
-                for at in range(SPAN // BLK)
+                jnp.where(
+                    pushed[block * (STEP // BLK) + at] == 1, fresh[at * BLK : (at + 1) * BLK], unsent
+                )
+                for at in range(STEP // BLK)
             ]
-            learned[part(block, 8)] = jnp.concatenate(marked, axis=0).astype(BF).reshape(8, 32, E)
-            return carry
-
-        lax.fori_loop(0, COLD // SPAN, cold_grad, 0)
-
+            groups_here = pl.ds(block * (STEP // 32), STEP // 32)
+            learned[groups_here] = jnp.concatenate(marked, axis=0).astype(BF).reshape(-1, 32, E)
         fetch.wait()
 
         def arrange(step, carry):
@@ -366,8 +357,16 @@
         wide[0:16, :] = small16[0].astype(F32)
         wide[16:32, :] = small16[1].astype(F32)
 
+        drain(allh.at[pl.ds(0, SHARDS - 1)], recvs.at[14])
+        eye = identity()
+        table_t[:, :HOT] = dot(eye, allh[...].reshape(HOT, E), NT).astype(BF)
+
+        def pool_hot(slot, carry):
+            pool_acc[part(slot, E), :] = dot(table_t[:, :HOT], counts[:HOT, part(slot, N)])
+            return carry
+
+        lax.fori_loop(0, SLOTS, pool_hot, 0)
         drain(arrived, recvs.at[13])
-        eye = identity()
 
         def merge(block, carry):
             rows = part(block, SPAN)
@@ -380,59 +379,56 @@
         lax.fori_loop(0, COLD // SPAN, merge, 0)
 
         def pool_cold(slot, carry):
-            pool_acc[part(slot, E), :] = dot(table_t[:, HOT:], counts[HOT:, part(slot, N)])
-            return carry
-
-        lax.fori_loop(0, SLOTS, pool_cold, 0)
-        drain(allh.at[pl.ds(0, SHARDS - 1)], recvs.at[14])
-        table_t[:, :HOT] = dot(eye, allh[...].reshape(HOT, E), NT).astype(BF)
-
-        def pool_hot(slot, carry):
             rows = part(slot, E)
             pooled_t[rows, :] = (
-                pool_acc[rows, :] + dot(table_t[:, :HOT], counts[:HOT, part(slot, N)])
+                pool_acc[rows, :] + dot(table_t[:, HOT:], counts[HOT:, part(slot, N)])
             ).astype(BF)
             return carry
 
-        lax.fori_loop(0, SLOTS, pool_hot, 0)
+        lax.fori_loop(0, SLOTS, pool_cold, 0)
+        ones = (lax.broadcasted_iota(jnp.int32, (16, N), 0) == 0).astype(F32).astype(BF)
+
+        def before(chunk, carry):
+            cols = part(chunk, 256)
+            pre_t[cols, :] = dot(weight[:, cols], pooled_t[...], TN) + dot(
+                wide[0:16, cols].astype(BF), ones, TN
+            )
+            return carry
+
+        lax.fori_loop(0, H // 256, before, 0)
         for axis in range(3):
             drain(rw[axis].at[pl.ds(0, 3)], recvs.at[9 + axis])
 
-        def squares(step, total):
-            value = allw[step // 16, lax.rem(step // 4, 4), lax.rem(step, 4)].astype(F32)
-            return total + value * value
-
-        total = lax.fori_loop(0, SHARDS, squares, jnp.zeros((PIECE, H), F32))
-        scale = (1.0 / math.sqrt(H)) / jnp.sqrt(jnp.sum(total, keepdims=True) / (H * H) + epsilon)
-
-        def update(step, carry):
-            rows = part(step, PIECE)
-            next_w[rows, :] = (
-                weight[rows, :].astype(F32) - allw[step // 16, lax.rem(step // 4, 4), lax.rem(step, 4)].astype(F32) * scale
-            ).astype(BF)
-            return carry
-
-        lax.fori_loop(0, SHARDS, update, 0)
-        weight_after[...] = next_w[part(me, PIECE), :]
-        piece_w2 = next_w.at[part(me, PIECE)]
         for axis in range(3):
             drain(plane[axis].at[pl.ds(0, 15)], sends.at[axis])
             drain(plane[axis].at[pl.ds(0, 15)], sends.at[3 + axis])
             drain(rw[axis].at[pl.ds(0, 3)], sends.at[6 + axis])
         drain(allh.at[pl.ds(0, SHARDS - 1)], sends.at[9])
+
+        def squares(step, total):
+            value = allw[step // 16, lax.rem(step // 4, 4), lax.rem(step, 4)].astype(F32)
+            return total + value * value
+
+        total = lax.fori_loop(0, SHARDS, squares, jnp.zeros((PIECE, H), F32))
+        scale = (1.0 / math.sqrt(H)) / jnp.sqrt(jnp.sum(total, keepdims=True) / (H * H) + epsilon)
+
+        weight_after[...] = (
+            weight[part(me, PIECE), :].astype(F32) - allw[coords].astype(F32) * scale
+        ).astype(BF)
+        piece_w[...] = weight_after[...]
         final_w = pltpu.make_async_remote_copy(
-            piece_w2, weight_after, sends.at[10], recvs.at[15], (0, me), MESH
+            piece_w, weight_after, sends.at[10], recvs.at[15], (0, me), MESH
         )
         final_h = pltpu.make_async_remote_copy(
             piece_h, hot_after, sends.at[11], recvs.at[16], (0, me), MESH
         )
         final_w.start()
         final_h.start()
-        ones = (lax.broadcasted_iota(jnp.int32, (16, N), 0) == 0).astype(F32).astype(BF)
 
         def score(chunk, logit):
             cols = part(chunk, 256)
-            pre = dot(next_w[:, cols], pooled_t[...], TN) + dot(wide[0:16, cols].astype(BF), ones, TN)
+            grad = allw[:, :, :, :, cols].reshape(H, 256)
+            pre = pre_t[cols, :] - dot(grad, pooled_t[...], TN) * scale
             hidden = (pre * sigmoid(pre)).astype(BF)
             return logit + dot(wide[16:32, cols].astype(BF), hidden)
 
@@ -478,7 +474,6 @@
             pltpu.VMEM((SHARDS, 32, E), BF),
             pltpu.VMEM((16, E), F32),
             pltpu.VMEM((32, H), F32),
-            pltpu.VMEM((H, H), BF),
             pltpu.VMEM((16, H), BF),
             pltpu.VMEM((16, H), BF),
             pltpu.VMEM((SHARDS, E), jnp.int32),

time: 70.9 us -> 65.4 us (0.922)
  Pallas kernels: 70 us -> 64.4 us
    pallas_call x1, Pallas kernels: 68.2 us -> 62.5 us  [run_round(): pl.pallas_call(round_kernel, out_shape=(jax.ShapeDtypeStruct((1, N), F32)...]
where the time goes in v4:
time: 65.4 us; the launch traced here: 65.2 us
  Pallas kernels  64.4 us (98%)
  between operations  0.82 us (1%)
    pallas_call x1, Pallas kernels, run_round(): pl.pallas_call(round_kernel, out_shape=(jax.ShapeDtypeStruct((1, N), F32)...  62.5 us
    pallas_call x1, Pallas kernels, hand_over(): pl.pallas_call(hand_over_kernel, out_shape=tuple((jax.ShapeDtypeStruct(ar...  1.88 us

profile of v4, /device:TPU:1, one launch (start us, length us, event | category | flops | bytes accessed | tf_op | source)
XLA Modules:
  0.0 65.2 jit_solution(13274057521897764437)
XLA Ops:
  0.6 62.5 %round.1 = (f32[1,512]{1,0:T(1,128)}, bf16[2048,128]{1,0:T(8,128)(2,1)}, bf16[16,128]{1,0:T(8,128)(2,1)}, bf16[16,1024]{1,0:T(8,128)(2,1)}) custom-call(s32[8,4,512]{2,1,0:T(4,128)} %bitcast.4, f32[512]{0:T(512)} %labels.1, bf16[1024,128]{1,0:T(8,128)(2,1)} %hot.1, bf16[2048,128]{1,0:T(8,128)(2,1)} %bitcast.3, bf16[1024,1024]{1,0:T(8,128)(2,1)} %weight.1, ...), custom_call_target="tpu_custom_call" | custom-call | tf_op jit(solution)/shard_map/round/pallas_call | solution.py:443
  63.2 1.9 %hand_over.1 = (f32[1,512]{1,0:T(1,128)}, bf16[2048,128]{1,0:T(8,128)(2,1)}, bf16[16,128]{1,0:T(8,128)(2,1)}, bf16[16,1024]{1,0:T(8,128)(2,1)}) custom-call(f32[1,512]{1,0:T(1,128)} %get-tuple-element.12.refs_0_, bf16[2048,128]{1,0:T(8,128)(2,1)} %get-tuple-element.13.refs_1_, bf16[16,128]{1,0:T(8,128)(2,1)} %get-tuple-element.14.refs_2_, ...), custom_call_target="tpu_custom_call" | custom-call | tf_op jit(solution)/shard_map/hand_over/pallas_call | solution.py:504

commit v5 on v4

--- a/solution.py
+++ b/solution.py
@@ -30,7 +30,7 @@
 BLK = 8
 SPAN = 256
 STEP = 512
-CHUNKS = ((0, 384), (384, 384), (768, 256))
+CHUNKS = ((0, 0, 384), (1, 384, 384), (2, 768, 256), (1, 0, 128))
 
 
 def dot(lhs, rhs, dims=NN):
@@ -102,13 +102,14 @@
     ids, labels, hot, cold, weight, bias_in, weight_out, owner, pushed,
     scores, cold_out, hot_after, weight_after,
     counts, table_t, pooled_t, pre_t, hidden_t, grad_t, grad_rows, pool_acc,
-    gw, rw0, rw1, rw2, line0, line1, line2, plane0, plane1, plane2, allw, gh, rh, allh, piece_w, piece_h, learned, outgoing, arrived, small, wide,
+    gw, rw0, rw1, rw2, rw3, line0, line1, line2, line3, plane0, plane1, plane2, plane3, allw, gh, gs, rs, allh, piece_w, piece_h, learned, outgoing, arrived, small, wide,
     bias, wout, source_rows, source, sends, recvs, local,
 ):
     role = lax.axis_index("role")
     me = lax.axis_index("shard")
     coords = (me // 16, lax.rem(me // 4, 4), lax.rem(me, 4))
-    rw, line, plane = (rw0, rw1, rw2), (line0, line1, line2), (plane0, plane1, plane2)
+    rw, line = (rw0, rw1, rw2, rw3), (line0, line1, line2, line3)
+    plane = (plane0, plane1, plane2, plane3)
     barrier = pltpu.get_barrier_semaphore()
     top = lax.broadcasted_iota(jnp.int32, (16, H), 0) == 0
     bias[...] = jnp.where(top, bias_in[...].reshape(1, H).astype(F32), 0.0).astype(BF)
@@ -188,43 +189,40 @@
         lax.fori_loop(0, H // 256, backward, 0)
         pl.semaphore_wait(barrier, SHARDS)
 
-        for axis, (first_col, width) in enumerate(CHUNKS):
-            cols = pl.ds(first_col, width)
-
-            def dense(chunk, carry):
-                rows = dot(pooled_t[part(chunk, 256), :], grad_t[cols, :], NT).astype(BF)
-                gw[chunk, :, :, :, cols] = rows.reshape(4, 4, PIECE, width)
-                return carry
-
-            lax.fori_loop(0, 4, dense, 0)
+        def send_line(chunk, ref, sem):
+            axis, first_col, width = CHUNKS[chunk]
             for step in range(4):
                 index = lax.rem(coords[axis] + step, 4)
                 pltpu.make_async_remote_copy(
-                    line_of(gw, axis, index, cols),
-                    rw[axis].at[coords[axis]],
-                    sends.at[0],
-                    recvs.at[axis],
+                    line_of(ref, axis, index, pl.ds(first_col, width)),
+                    rw[chunk].at[coords[axis]],
+                    sem,
+                    recvs.at[chunk],
                     (1, on_line(coords, axis, index)),
                     MESH,
                 ).start()
 
+        for chunk in range(3):
+            _, first_col, width = CHUNKS[chunk]
+            cols = pl.ds(first_col, width)
+
+            def dense(block, carry):
+                rows = dot(pooled_t[part(block, 256), :], grad_t[cols, :], NT).astype(BF)
+                gw[block, :, :, :, cols] = rows.reshape(4, 4, PIECE, width)
+                return carry
+
+            lax.fori_loop(0, 4, dense, 0)
+            send_line(chunk, gw, sends.at[0])
+
         def rows_grad(slot, carry):
             grad_rows[:, part(slot, N)] = dot(weight[part(slot, E), :], grad_t[...]).astype(BF)
             return carry
 
         lax.fori_loop(0, SLOTS, rows_grad, 0)
-        for row in range(8):
-            small[row : row + 1, :] = wide[0:1, row * E : (row + 1) * E]
-            small[row + 8 : row + 9, :] = wide[16:17, row * E : (row + 1) * E]
-        small_piece = jnp.broadcast_to(small[...].astype(BF)[None], (16, PIECE, E))
-
         for block in range(HOT // STEP):
             rows = dot(counts[block * STEP : (block + 1) * STEP, :], grad_rows[...], NT).astype(BF)
-            at = pl.ds(block * (STEP // PIECE), STEP // PIECE)
-            gh[at, 0:PIECE, :] = rows.reshape(STEP // PIECE, PIECE, E)
-        for block in range(4):
-            gh[block * 16 : block * 16 + 16, PIECE : 2 * PIECE, :] = small_piece
-        send_all(0, lambda to: gh.at[to], rh.at[me], sends.at[1], recvs.at[12])
+            gh[block * 2 : block * 2 + 2] = rows.reshape(2, 4, 4, PIECE, E)
+        send_line(3, gh, sends.at[1])
         for block in range(COLD // STEP):
             rows = pl.ds(block * STEP, STEP)
             grad = dot(counts[pl.ds(HOT + block * STEP, STEP), :], grad_rows[...], NT)
@@ -245,12 +243,18 @@
             return carry
 
         lax.fori_loop(0, SHARDS, arrange, 0)
-        send_all(0, lambda to: outgoing.at[to], arrived.at[me], sends.at[2], recvs.at[13])
+        send_all(0, lambda to: outgoing.at[to], arrived.at[me], sends.at[2], recvs.at[16])
+        for row in range(8):
+            small[row : row + 1, :] = wide[0:1, row * E : (row + 1) * E]
+            small[row + 8 : row + 9, :] = wide[16:17, row * E : (row + 1) * E]
+        gs[...] = small[...].astype(BF)
+        send_all(0, lambda to: gs, rs.at[me], sends.at[3], recvs.at[17])
         drain(gw, sends.at[0])
+        drain(rs, sends.at[3])
         drain(gh, sends.at[1])
         drain(outgoing, sends.at[2])
-        drain(weight_after, recvs.at[15])
-        drain(hot_after, recvs.at[16])
+        drain(weight_after, recvs.at[18])
+        drain(hot_after, recvs.at[19])
 
     @pl.when(role == 1)
     def _():
@@ -266,82 +270,135 @@
 
         lax.fori_loop(0, SLOTS, count_slot, 0)
         pl.semaphore_wait(barrier, SHARDS)
-        for axis, (first_col, width) in enumerate(CHUNKS):
-            drain(rw[axis], recvs.at[axis])
-
-            def add_line(step, carry):
+        eye = identity()
+        def add_line(chunk):
+            axis = CHUNKS[chunk][0]
+            drain(rw[chunk], recvs.at[chunk])
+
+            def add(step, carry):
                 at = (step // 4, lax.rem(step, 4))
-                total = sum(rw[axis][(source, *at)].astype(F32) for source in range(4))
-                line[axis][step] = total.astype(BF)
+                total = sum(rw[chunk][(source, *at)].astype(F32) for source in range(4))
+                line[chunk][step] = total.astype(BF)
                 return carry
 
-            lax.fori_loop(0, 16, add_line, 0)
+            lax.fori_loop(0, 16, add, 0)
             own = plane_index(coords, axis)
 
-            def send_plane(step, carry):
+            def send(step, carry):
                 index = lax.rem(own + step, 16)
                 pltpu.make_async_remote_copy(
-                    line[axis].at[index],
-                    plane[axis].at[own],
-                    sends.at[axis],
-                    recvs.at[3 + axis],
+                    line[chunk].at[index],
+                    plane[chunk].at[own],
+                    sends.at[chunk],
+                    recvs.at[4 + chunk],
                     (1, in_plane(coords, axis, index)),
                     MESH,
                 ).start()
                 return carry
 
-            lax.fori_loop(1, 16, send_plane, 0)
-            plane[axis][own] = line[axis][own]
-        for axis, (first_col, width) in enumerate(CHUNKS):
+            lax.fori_loop(1, 16, send, 0)
+            plane[chunk][own] = line[chunk][own]
+
+        def add_plane(chunk):
+            axis, first_col, width = CHUNKS[chunk]
             cols = pl.ds(first_col, width)
-            drain(plane[axis].at[pl.ds(0, 15)], recvs.at[3 + axis])
+            drain(plane[chunk].at[pl.ds(0, 15)], recvs.at[4 + chunk])
             total = lax.fori_loop(
                 0,
                 16,
-                lambda step, total: total + plane[axis][step].astype(F32),
+                lambda step, total: total + plane[chunk][step].astype(F32),
                 jnp.zeros((PIECE, width), F32),
-            ).astype(BF)
-            piece_w[:, cols] = total
-            allw[(*coords, slice(None), cols)] = total
+            )
+            piece, whole = (piece_w, allw) if chunk < 3 else (piece_h, allh)
+            if chunk == 3:
+                total = step_rows(hot[part(me, PIECE), :], total)
+                hot_after[...] = total.astype(BF)
+            piece[:, cols] = total.astype(BF)
+            whole[(*coords, slice(None), cols)] = total.astype(BF)
             own = plane_index(coords, axis)
 
-            def spread_plane(step, carry):
+            def send(step, carry):
                 pltpu.make_async_remote_copy(
-                    piece_w.at[:, cols],
-                    allw.at[(*coords, slice(None), cols)],
-                    sends.at[3 + axis],
-                    recvs.at[6 + axis],
+                    piece.at[:, cols],
+                    whole.at[(*coords, slice(None), cols)],
+                    sends.at[4 + chunk],
+                    recvs.at[8 + chunk],
                     (1, in_plane(coords, axis, lax.rem(own + step, 16))),
                     MESH,
                 ).start()
                 return carry
 
-            lax.fori_loop(1, 16, spread_plane, 0)
-        drain(rh, recvs.at[12])
-        total = lax.fori_loop(
-            0,
-            SHARDS,
-            lambda step, total: total + rh[step].astype(F32),
-            jnp.zeros((2 * PIECE, E), F32),
-        )
-        piece_h[...] = step_rows(hot[part(me, PIECE), :], total[:PIECE]).astype(BF)
-        send_all(1, lambda to: piece_h, allh.at[me], sends.at[9], recvs.at[14])
-        allh[me] = piece_h[...]
-        hot_after[...] = piece_h[...]
-        for axis, (first_col, width) in enumerate(CHUNKS):
+            lax.fori_loop(1, 16, send, 0)
+
+        def spread_line(chunk):
+            axis, first_col, width = CHUNKS[chunk]
             cols = pl.ds(first_col, width)
-            drain(plane[axis].at[pl.ds(0, 15)], recvs.at[6 + axis])
+            whole = allw if chunk < 3 else allh
+            drain(plane[chunk].at[pl.ds(0, 15)], recvs.at[8 + chunk])
             for step in range(1, 4):
                 index = lax.rem(coords[axis] + step, 4)
                 pltpu.make_async_remote_copy(
-                    line_of(allw, axis, coords[axis], cols),
-                    line_of(allw, axis, coords[axis], cols),
-                    sends.at[6 + axis],
-                    recvs.at[9 + axis],
+                    line_of(whole, axis, coords[axis], cols),
+                    line_of(whole, axis, coords[axis], cols),
+                    sends.at[8 + chunk],
+                    recvs.at[12 + chunk],
                     (1, on_line(coords, axis, index)),
                     MESH,
                 ).start()
-        sums = total[PIECE:]
+
+        for chunk in range(3):
+            add_line(chunk)
+        for chunk in (3,):
+            add_line(chunk)
+        for chunk in range(3):
+            add_plane(chunk)
+        for chunk in (3,):
+            add_plane(chunk)
+        for chunk in (3, 0, 1, 2):
+            spread_line(chunk)
+        drain(arrived, recvs.at[16])
+
+        def merge(block, carry):
+            rows = part(block, SPAN)
+            came = arrived[part(block, 8)].reshape(SPAN, E)
+            fresh = jnp.where(came < unsent * 0.5, came, cold[rows, :])
+            cold_out[rows, :] = fresh
+            table_t[:, pl.ds(pl.multiple_of(HOT + block * SPAN, SPAN), SPAN)] = dot(eye, fresh, NT).astype(BF)
+            return carry
+
+        lax.fori_loop(0, COLD // SPAN, merge, 0)
+
+        def pool_cold(slot, carry):
+            pool_acc[part(slot, E), :] = dot(table_t[:, HOT:], counts[HOT:, part(slot, N)])
+            return carry
+
+        lax.fori_loop(0, SLOTS, pool_cold, 0)
+        drain(rw[3].at[pl.ds(0, 3)], recvs.at[15])
+        table_t[:, :HOT] = dot(eye, allh[...].reshape(HOT, E), NT).astype(BF)
+
+        def pool_hot(slot, carry):
+            rows = part(slot, E)
+            pooled_t[rows, :] = (
+                pool_acc[rows, :] + dot(table_t[:, :HOT], counts[:HOT, part(slot, N)])
+            ).astype(BF)
+            return carry
+
+        lax.fori_loop(0, SLOTS, pool_hot, 0)
+        ones = (lax.broadcasted_iota(jnp.int32, (16, N), 0) == 0).astype(F32).astype(BF)
+
+        def before(chunk, carry):
+            cols = part(chunk, 256)
+            pre_t[cols, :] = dot(weight[:, cols], pooled_t[...], TN)
+            return carry
+
+        lax.fori_loop(0, H // 256, before, 0)
+        drain(rs, recvs.at[17])
+        sums = lax.fori_loop(
+            0,
+            SHARDS,
+            lambda step, total: total + rs[step].astype(F32),
+            jnp.zeros((16, E), F32),
+        )
         bias_sum, out_sum = sums[:8], sums[8:]
         bias_scale = 0.5 / jnp.sqrt(jnp.mean(bias_sum * bias_sum, keepdims=True) + epsilon)
         out_scale = (1.0 / math.sqrt(H)) / jnp.sqrt(jnp.mean(out_sum * out_sum, keepdims=True) + epsilon)
@@ -357,53 +414,13 @@
         wide[0:16, :] = small16[0].astype(F32)
         wide[16:32, :] = small16[1].astype(F32)
 
-        drain(allh.at[pl.ds(0, SHARDS - 1)], recvs.at[14])
-        eye = identity()
-        table_t[:, :HOT] = dot(eye, allh[...].reshape(HOT, E), NT).astype(BF)
-
-        def pool_hot(slot, carry):
-            pool_acc[part(slot, E), :] = dot(table_t[:, :HOT], counts[:HOT, part(slot, N)])
-            return carry
-
-        lax.fori_loop(0, SLOTS, pool_hot, 0)
-        drain(arrived, recvs.at[13])
-
-        def merge(block, carry):
-            rows = part(block, SPAN)
-            came = arrived[part(block, 8)].reshape(SPAN, E)
-            fresh = jnp.where(came < unsent * 0.5, came, cold[rows, :])
-            cold_out[rows, :] = fresh
-            table_t[:, pl.ds(pl.multiple_of(HOT + block * SPAN, SPAN), SPAN)] = dot(eye, fresh, NT).astype(BF)
-            return carry
-
-        lax.fori_loop(0, COLD // SPAN, merge, 0)
-
-        def pool_cold(slot, carry):
-            rows = part(slot, E)
-            pooled_t[rows, :] = (
-                pool_acc[rows, :] + dot(table_t[:, HOT:], counts[HOT:, part(slot, N)])
-            ).astype(BF)
-            return carry
-
-        lax.fori_loop(0, SLOTS, pool_cold, 0)
-        ones = (lax.broadcasted_iota(jnp.int32, (16, N), 0) == 0).astype(F32).astype(BF)
-
-        def before(chunk, carry):
-            cols = part(chunk, 256)
-            pre_t[cols, :] = dot(weight[:, cols], pooled_t[...], TN) + dot(
-                wide[0:16, cols].astype(BF), ones, TN
-            )
-            return carry
-
-        lax.fori_loop(0, H // 256, before, 0)
-        for axis in range(3):
-            drain(rw[axis].at[pl.ds(0, 3)], recvs.at[9 + axis])
-
-        for axis in range(3):
-            drain(plane[axis].at[pl.ds(0, 15)], sends.at[axis])
-            drain(plane[axis].at[pl.ds(0, 15)], sends.at[3 + axis])
-            drain(rw[axis].at[pl.ds(0, 3)], sends.at[6 + axis])
-        drain(allh.at[pl.ds(0, SHARDS - 1)], sends.at[9])
+        for chunk in range(3):
+            drain(rw[chunk].at[pl.ds(0, 3)], recvs.at[12 + chunk])
+
+        for chunk in range(4):
+            drain(plane[chunk].at[pl.ds(0, 15)], sends.at[chunk])
+            drain(plane[chunk].at[pl.ds(0, 15)], sends.at[4 + chunk])
+            drain(rw[chunk].at[pl.ds(0, 3)], sends.at[8 + chunk])
 
         def squares(step, total):
             value = allw[step // 16, lax.rem(step // 4, 4), lax.rem(step, 4)].astype(F32)
@@ -417,10 +434,10 @@
         ).astype(BF)
         piece_w[...] = weight_after[...]
         final_w = pltpu.make_async_remote_copy(
-            piece_w, weight_after, sends.at[10], recvs.at[15], (0, me), MESH
+            piece_w, weight_after, sends.at[12], recvs.at[18], (0, me), MESH
         )
         final_h = pltpu.make_async_remote_copy(
-            piece_h, hot_after, sends.at[11], recvs.at[16], (0, me), MESH
+            piece_h, hot_after, sends.at[13], recvs.at[19], (0, me), MESH
         )
         final_w.start()
         final_h.start()
@@ -429,6 +446,7 @@
             cols = part(chunk, 256)
             grad = allw[:, :, :, :, cols].reshape(H, 256)
             pre = pre_t[cols, :] - dot(grad, pooled_t[...], TN) * scale
+            pre = pre + dot(wide[0:16, cols].astype(BF), ones, TN)
             hidden = (pre * sigmoid(pre)).astype(BF)
             return logit + dot(wide[16:32, cols].astype(BF), hidden)
 
@@ -460,13 +478,14 @@
             pltpu.VMEM((E, SLOTS * N), BF),
             pltpu.VMEM((H, N), F32),
             pltpu.VMEM((4, 4, 4, PIECE, H), BF),
-            *[pltpu.VMEM((4, 4, 4, PIECE, width), BF) for _, width in CHUNKS],
-            *[pltpu.VMEM((16, PIECE, width), BF) for _, width in CHUNKS],
-            *[pltpu.VMEM((16, PIECE, width), BF) for _, width in CHUNKS],
+            *[pltpu.VMEM((4, 4, 4, PIECE, width), BF) for _, _, width in CHUNKS],
+            *[pltpu.VMEM((16, PIECE, width), BF) for _, _, width in CHUNKS],
+            *[pltpu.VMEM((16, PIECE, width), BF) for _, _, width in CHUNKS],
             pltpu.VMEM((4, 4, 4, PIECE, H), BF),
-            pltpu.VMEM((SHARDS, 2 * PIECE, E), BF),
-            pltpu.VMEM((SHARDS, 2 * PIECE, E), BF),
-            pltpu.VMEM((SHARDS, PIECE, E), BF),
+            pltpu.VMEM((4, 4, 4, PIECE, E), BF),
+            pltpu.VMEM((16, E), BF),
+            pltpu.VMEM((SHARDS, 16, E), BF),
+            pltpu.VMEM((4, 4, 4, PIECE, E), BF),
             pltpu.VMEM((PIECE, H), BF),
             pltpu.VMEM((PIECE, E), BF),
             pltpu.VMEM((SHARDS, 32, E), BF),
@@ -478,8 +497,8 @@
             pltpu.VMEM((16, H), BF),
             pltpu.VMEM((SHARDS, E), jnp.int32),
             pltpu.SMEM((SHARDS, E), jnp.int32),
-            pltpu.SemaphoreType.DMA((12,)),
-            pltpu.SemaphoreType.DMA((17,)),
+            pltpu.SemaphoreType.DMA((14,)),
+            pltpu.SemaphoreType.DMA((20,)),
             pltpu.SemaphoreType.DMA((1,)),
         ],
         compiler_params=pltpu.CompilerParams(

time: 65.4 us -> 64.3 us (0.983)
  Pallas kernels: 64.4 us -> 63.3 us
    pallas_call x1, Pallas kernels: 62.5 us -> 61.4 us  [run_round(): pl.pallas_call(round_kernel, out_shape=(jax.ShapeDtypeStruct((1, N), F32)...]
where the time goes in v5:
time: 64.3 us; the launch traced here: 64.1 us
  Pallas kernels  63.3 us (98%)
  between operations  0.82 us (1%)
    pallas_call x1, Pallas kernels, run_round(): pl.pallas_call(round_kernel, out_shape=(jax.ShapeDtypeStruct((1, N), F32)...  61.4 us
    pallas_call x1, Pallas kernels, hand_over(): pl.pallas_call(hand_over_kernel, out_shape=tuple((jax.ShapeDtypeStruct(ar...  1.88 us

profile of v5, /device:TPU:1, one launch (start us, length us, event | category | flops | bytes accessed | tf_op | source)
XLA Modules:
  0.0 64.1 jit_solution(3958765460413859494)
XLA Ops:
  0.6 61.4 %round.1 = (f32[1,512]{1,0:T(1,128)}, bf16[2048,128]{1,0:T(8,128)(2,1)}, bf16[16,128]{1,0:T(8,128)(2,1)}, bf16[16,1024]{1,0:T(8,128)(2,1)}) custom-call(s32[8,4,512]{2,1,0:T(4,128)} %bitcast.4, f32[512]{0:T(512)} %labels.1, bf16[1024,128]{1,0:T(8,128)(2,1)} %hot.1, bf16[2048,128]{1,0:T(8,128)(2,1)} %bitcast.3, bf16[1024,1024]{1,0:T(8,128)(2,1)} %weight.1, ...), custom_call_target="tpu_custom_call" | custom-call | tf_op jit(solution)/shard_map/round/pallas_call | solution.py:461
  62.1 1.9 %hand_over.1 = (f32[1,512]{1,0:T(1,128)}, bf16[2048,128]{1,0:T(8,128)(2,1)}, bf16[16,128]{1,0:T(8,128)(2,1)}, bf16[16,1024]{1,0:T(8,128)(2,1)}) custom-call(f32[1,512]{1,0:T(1,128)} %get-tuple-element.12.refs_0_, bf16[2048,128]{1,0:T(8,128)(2,1)} %get-tuple-element.13.refs_1_, bf16[16,128]{1,0:T(8,128)(2,1)} %get-tuple-element.14.refs_2_, ...), custom_call_target="tpu_custom_call" | custom-call | tf_op jit(solution)/shard_map/hand_over/pallas_call | solution.py:523

commit v6 on v5

--- a/solution.py
+++ b/solution.py
@@ -172,7 +172,7 @@
             hidden_t[cols, :] = hidden
             return logit + dot(wout[:, cols], hidden)
 
-        logit = lax.fori_loop(0, H // 256, forward, jnp.zeros((16, N), F32))
+        logit = lax.fori_loop(0, H // 256, forward, jnp.zeros((16, N), F32), unroll=True)
         scores[...] = logit[0:1]
         slope = jnp.where(first, sigmoid(logit) - labels[...].reshape(1, N), 0.0).astype(BF)
 
@@ -186,7 +186,7 @@
             wide[16:32, cols] = dot(slope, hidden_t[cols, :], NT)
             return carry
 
-        lax.fori_loop(0, H // 256, backward, 0)
+        lax.fori_loop(0, H // 256, backward, 0, unroll=True)
         pl.semaphore_wait(barrier, SHARDS)
 
         def send_line(chunk, ref, sem):
@@ -211,7 +211,7 @@
                 gw[block, :, :, :, cols] = rows.reshape(4, 4, PIECE, width)
                 return carry
 
-            lax.fori_loop(0, 4, dense, 0)
+            lax.fori_loop(0, 4, dense, 0, unroll=True)
             send_line(chunk, gw, sends.at[0])
 
         def rows_grad(slot, carry):
@@ -281,7 +281,7 @@
                 line[chunk][step] = total.astype(BF)
                 return carry
 
-            lax.fori_loop(0, 16, add, 0)
+            lax.fori_loop(0, 16, add, 0, unroll=4)
             own = plane_index(coords, axis)
 
             def send(step, carry):
@@ -366,7 +366,7 @@
             table_t[:, pl.ds(pl.multiple_of(HOT + block * SPAN, SPAN), SPAN)] = dot(eye, fresh, NT).astype(BF)
             return carry
 
-        lax.fori_loop(0, COLD // SPAN, merge, 0)
+        lax.fori_loop(0, COLD // SPAN, merge, 0, unroll=True)
 
         def pool_cold(slot, carry):
             pool_acc[part(slot, E), :] = dot(table_t[:, HOT:], counts[HOT:, part(slot, N)])
@@ -391,7 +391,7 @@
             pre_t[cols, :] = dot(weight[:, cols], pooled_t[...], TN)
             return carry
 
-        lax.fori_loop(0, H // 256, before, 0)
+        lax.fori_loop(0, H // 256, before, 0, unroll=True)
         drain(rs, recvs.at[17])
         sums = lax.fori_loop(
             0,
@@ -426,7 +426,7 @@
             value = allw[step // 16, lax.rem(step // 4, 4), lax.rem(step, 4)].astype(F32)
             return total + value * value
 
-        total = lax.fori_loop(0, SHARDS, squares, jnp.zeros((PIECE, H), F32))
+        total = lax.fori_loop(0, SHARDS, squares, jnp.zeros((PIECE, H), F32), unroll=8)
         scale = (1.0 / math.sqrt(H)) / jnp.sqrt(jnp.sum(total, keepdims=True) / (H * H) + epsilon)
 
         weight_after[...] = (
@@ -450,7 +450,7 @@
             hidden = (pre * sigmoid(pre)).astype(BF)
             return logit + dot(wide[16:32, cols].astype(BF), hidden)
 
-        scores[...] = lax.fori_loop(0, H // 256, score, jnp.zeros((16, N), F32))[0:1]
+        scores[...] = lax.fori_loop(0, H // 256, score, jnp.zeros((16, N), F32), unroll=True)[0:1]
         final_w.wait_send()
         final_h.wait_send()
 

time: 64.3 us -> 58.2 us (0.905)
  Pallas kernels: 63.3 us -> 57.2 us
    pallas_call x1, Pallas kernels: 61.4 us -> 55.3 us  [run_round(): pl.pallas_call(round_kernel, out_shape=(jax.ShapeDtypeStruct((1, N), F32)...]
where the time goes in v6:
time: 58.2 us; the launch traced here: 58 us
  Pallas kernels  57.2 us (98%)
  between operations  0.82 us (1%)
    pallas_call x1, Pallas kernels, run_round(): pl.pallas_call(round_kernel, out_shape=(jax.ShapeDtypeStruct((1, N), F32)...  55.3 us
    pallas_call x1, Pallas kernels, hand_over(): pl.pallas_call(hand_over_kernel, out_shape=tuple((jax.ShapeDtypeStruct(ar...  1.88 us

profile of v6, /device:TPU:1, one launch (start us, length us, event | category | flops | bytes accessed | tf_op | source)
XLA Modules:
  0.0 58.0 jit_solution(2898808975470339219)
XLA Ops:
  0.6 55.3 %round.1 = (f32[1,512]{1,0:T(1,128)}, bf16[2048,128]{1,0:T(8,128)(2,1)}, bf16[16,128]{1,0:T(8,128)(2,1)}, bf16[16,1024]{1,0:T(8,128)(2,1)}) custom-call(s32[8,4,512]{2,1,0:T(4,128)} %bitcast.4, f32[512]{0:T(512)} %labels.1, bf16[1024,128]{1,0:T(8,128)(2,1)} %hot.1, bf16[2048,128]{1,0:T(8,128)(2,1)} %bitcast.3, bf16[1024,1024]{1,0:T(8,128)(2,1)} %weight.1, ...), custom_call_target="tpu_custom_call" | custom-call | tf_op jit(solution)/shard_map/round/pallas_call | solution.py:461
  55.9 1.9 %hand_over.1 = (f32[1,512]{1,0:T(1,128)}, bf16[2048,128]{1,0:T(8,128)(2,1)}, bf16[16,128]{1,0:T(8,128)(2,1)}, bf16[16,1024]{1,0:T(8,128)(2,1)}) custom-call(f32[1,512]{1,0:T(1,128)} %get-tuple-element.12.refs_0_, bf16[2048,128]{1,0:T(8,128)(2,1)} %get-tuple-element.13.refs_1_, bf16[16,128]{1,0:T(8,128)(2,1)} %get-tuple-element.14.refs_2_, ...), custom_call_target="tpu_custom_call" | custom-call | tf_op jit(solution)/shard_map/hand_over/pallas_call | solution.py:523
